TPU v7x, 256 devices: a whole 4x4x8 slice. The times are simulated.
256 devices in a mesh: grp: 4 (over x), row: 4 (over y_lo, core), col: 16 (over y_hi, z).
Axes of the slice: x: 4, y: 4 (y_hi: 2, y_lo: 2; y = y_hi * 2 + y_lo), z: 8, core: 2. Of those that a mesh axis runs over, the one named last changes fastest.
Arguments:
- acts: bfloat16 [16, 1024, 4096], P('grp', None, 'row'), may hold values from -6 to 6
- grads: bfloat16 [16, 1024, 4096], P('grp', None, 'col'), may hold values from -6 to 6
- act_basis: bfloat16 [4096, 4096], P('row', 'col'), may hold values from -0.09375 to 0.09375
- grad_basis: bfloat16 [4096, 4096], P('col', ('grp', 'row')), may hold values from -0.09375 to 0.09375
Outputs:
- eigenvalues: float32 [4096, 4096], P(('grp', 'row'), 'col')
All inputs are finite; a program needn't handle non-finite values.
Results may differ from a plain program's by a relative error of at most 0.002.
Values may be sent and summed in bfloat16 or wider, within the bound.
A program may use at most 128 MiB of HBM per device.

v0:
```python
import jax
import jax.numpy as jnp
from jax import lax
from jax.sharding import PartitionSpec as P


def per_device(acts, grads, act_basis, grad_basis):
    seq_dev, length, grad_width = grads.shape
    total_rows = seq_dev * length
    grad_flat = grads.reshape(total_rows, grad_width)
    act_flat = acts.reshape(total_rows, acts.shape[2])
    act_terms = jnp.dot(act_flat, act_basis, preferred_element_type=jnp.float32)
    rotated_acts = lax.psum(act_terms, "row").astype(jnp.bfloat16)
    groups = lax.axis_size("grp")
    scale = 1.0 / float(seq_dev * groups * length)
    panel = lax.all_gather(grad_basis, "grp", axis=1, tiled=True)
    shares = lax.psum_scatter(
        jnp.dot(grad_flat, panel, preferred_element_type=jnp.float32),
        "col",
        scatter_dimension=0,
        tiled=True,
    )
    rotated_grads = lax.all_gather(shares.astype(jnp.bfloat16), "col", axis=0, tiled=True)
    grad_seqs = rotated_grads.reshape(seq_dev, length, rotated_grads.shape[1])
    act_seqs = rotated_acts.reshape(seq_dev, length, rotated_acts.shape[1])
    tiles = jnp.einsum("slr,slc->src", grad_seqs, act_seqs, preferred_element_type=jnp.float32)
    return lax.psum_scatter(
        jnp.sum(tiles * tiles, axis=0) * scale, "grp", scatter_dimension=0, tiled=True
    )


def solution(mesh):
    placed = (
        P("grp", None, "row"),
        P("grp", None, "col"),
        P("row", "col"),
        P("col", ("grp", "row")),
    )
    return jax.shard_map(
        per_device, mesh=mesh, in_specs=placed, out_specs=P(("grp", "row"), "col"), check_vma=False
    )
```

profile of v0, /device:TPU:1, one launch (start us, length us, event | category | flops | bytes accessed | tf_op | source)
XLA Modules:
  0.0 523.6 jit_solution(14958704860274133293)
XLA Ops:
  6.5 0.0 copy-start
  6.5 0.0 reduce-scatter.3.cloned.1.call-start
  6.5 12.7 %all_gather.6 = bf16[256,1024]{1,0:T(8,128)(2,1)S(1)} all-gather(bf16[256,256]{1,0:T(8,128)(2,1)} %param.7), channel_id=1, replica_groups=mesh['grp'=4,'row'=4,'col'=16] {'grp'}, dimensions={1}, use_global_device_ids=true | all-gather | bytes 655360 | tf_op jit(solution)/shard_map/all_gather | solution.py:16
  19.2 0.0 copy-done
  19.2 8.1 %fusion = f32[4096,1024]{1,0:T(8,128)} fusion(bf16[4096,256]{1,0:T(8,128)(2,1)S(1)} %bitcast.10, bf16[256,1024]{1,0:T(8,128)(2,1)S(1)} %all_gather.6), kind=kOutput, calls=%fused_computation.2 | convolution fusion | flops 2147483648 | bytes 19398656 | tf_op jit(solution)/shard_map/dot_general | solution.py:18
  27.3 0.0 copy-start.1
  27.3 0.0 reduce-scatter.3.cloned.1.call-update
  27.3 0.0 all-gather.2.cloned.1.call-start
  27.3 289.6 %reduce-scatter.3.cloned.1.call-done = f32[256,1024]{1,0:T(8,128)} async-done(((f32[4096,1024]{1,0:T(8,128)}), f32[256,1024]{1,0:T(8,128)}) %reduce-scatter.3.cloned.1.call-update) | async-done | bytes 1048592 | tf_op jit(solution)/shard_map/reduce_scatter | solution.py:17
  317.0 2.1 convert_element_type.6
  319.1 0.0 all-gather.2.cloned.1.call-update
  319.1 0.0 reduce-scatter.5.cloned.1.call-start
  319.2 0.0 copy-done.1
  319.2 7.7 %fusion.1 = f32[4096,256]{1,0:T(8,128)} fusion(bf16[4096,1024]{1,0:T(8,128)(2,1)} %bitcast.12, bf16[1024,256]{1,0:T(8,128)(2,1)S(1)} %copy-done.1), kind=kOutput, calls=%fused_computation.3 | convolution fusion | flops 2147483648 | bytes 13107200 | tf_op jit(solution)/shard_map/dot_general | solution.py:12
  326.9 110.8 %all-reduce.1 = bf16[4096,256]{1,0:T(8,128)(2,1)} all-reduce(f32[4096,256]{1,0:T(8,128)} %fusion.1), channel_id=1, replica_groups=mesh['grp'=4,'row'=4,'col'=16] {'row'}, use_global_device_ids=true, to_apply=%region_1.0 | all-reduce | flops 1048576 | bytes 6291456 | tf_op jit(solution)/shard_map/psum | solution.py:13
  437.7 47.2 %all-gather.2.cloned.1.call-done = bf16[4096,1024]{1,0:T(8,128)(2,1)} async-done(((bf16[256,1024]{1,0:T(8,128)(2,1)}), bf16[4096,1024]{1,0:T(8,128)(2,1)}) %all-gather.2.cloned.1.call-update) | async-done | bytes 8388624 | tf_op jit(solution)/shard_map/all_gather | solution.py:23
  485.0 7.0 %multiply_reduce_fusion = f32[1024,256]{1,0:T(8,128)S(1)} fusion(bf16[4,1024,1024]{2,1,0:T(8,128)(2,1)} %bitcast.13, bf16[4,1024,256]{2,1,0:T(8,128)(2,1)} %bitcast.11), kind=kOutput, calls=%fused_computation | convolution fusion | flops 2149318656 | bytes 11534336 | tf_op jit(solution)/shard_map/slr,slc->src/dot_general | solution.py:26
  492.0 1.1 broadcast_multiply_fusion
  493.1 0.0 reduce-scatter.5.cloned.1.call-update
  493.1 24.0 %reduce-scatter.5.cloned.1.call-done = f32[256,256]{1,0:T(8,128)} async-done(((f32[1024,256]{1,0:T(8,128)}), f32[256,256]{1,0:T(8,128)}) %reduce-scatter.5.cloned.1.call-update) | async-done | bytes 262160 | tf_op jit(solution)/shard_map/reduce_scatter | solution.py:27
Async XLA Ops:
  6.5 12.7 %copy-start = (bf16[4,1024,256]{2,1,0:T(8,128)(2,1)S(1)}, bf16[4,1024,256]{2,1,0:T(8,128)(2,1)}, u32[]{:S(2)}) copy-start(bf16[4,1024,256]{2,1,0:T(8,128)(2,1)} %param.5) | copy-start | bytes 6291460
  6.5 310.5 %reduce-scatter.3.cloned.1.call-start = ((), (), s32[]{:S(2)}) async-start(), calls=%async_computation.2 | async-start | bytes 17825792 | tf_op jit(solution)/shard_map/reduce_scatter | solution.py:17
  27.3 291.9 %copy-start.1 = (bf16[1024,256]{1,0:T(8,128)(2,1)S(1)}, bf16[1024,256]{1,0:T(8,128)(2,1)}, u32[]{:S(2)}) copy-start(bf16[1024,256]{1,0:T(8,128)(2,1)} %param.6) | copy-start | bytes 1572868
  27.3 457.7 %all-gather.2.cloned.1.call-start = ((), (), s32[]{:S(2)}) async-start(), calls=%async_computation.3 | async-start | bytes 8912896 | tf_op jit(solution)/shard_map/all_gather | solution.py:23
  319.1 197.9 %reduce-scatter.5.cloned.1.call-start = ((), (), s32[]{:S(2)}) async-start(), calls=%async_computation.4 | async-start | bytes 1310720 | tf_op jit(solution)/shard_map/reduce_scatter | solution.py:27
Sparse Core Ops, SparseCore 0:
  27.4 289.5 reduce-scatter.2
  319.6 165.3 all-gather.1
  493.2 23.8 reduce-scatter.4
where the time goes:
time: 524 us
  waiting for transfers between devices  361 us (69%)
  blocking collectives  124 us (24%)
  matrix products  22.8 us (4%)
  between operations  13.1 us (2%)
    reduce_scatter x1, waiting for transfers between devices, per_device(): lax.psum_scatter(jnp.dot(grad_flat, panel, preferred_element_type=jnp.flo...  290 us
    psum x1, blocking collectives, per_device(): rotated_acts = lax.psum(act_terms, 'row').astype(jnp.bfloat16)  111 us
    all_gather x1, waiting for transfers between devices, per_device(): lax.all_gather(shares.astype(jnp.bfloat16), 'col', axis=0, tiled=True)  47.2 us
    reduce_scatter x1, waiting for transfers between devices, per_device(): lax.psum_scatter(jnp.sum(tiles * tiles, axis=0) * scale, 'grp', scatter_d...  24 us
    all_gather x1, blocking collectives, per_device(): panel = lax.all_gather(grad_basis, 'grp', axis=1, tiled=True)  12.7 us
  transfers between devices with their start and end apart: 3, of which 3 were waited for; matrix products, arithmetic and copies ran while one was open for 1% of the time, Pallas kernels for 0%

commit v1 on v0

v1 whole, which is shorter than its diff:
```python
import jax
import jax.numpy as jnp
from jax import lax
from jax.experimental import pallas as pl
from jax.experimental.pallas import tpu as pltpu
from jax.sharding import PartitionSpec as P

MESH = pl.DeviceIdType.MESH
F32 = jnp.float32
BF16 = jnp.bfloat16


def kernel(acts, grads, actb, gradb, out, *scratch):
    (gsrc, xs, gq, bas, gp, gs, gr, gt, av, actv, ap, ar, abs_, abr, aown, axs, agat,
     ob, obr, oacc, zsnd, fin,
     ld, xs_s, xs_r, za_s, za_r, xg_s, xg_r, bz_s, bz_r, bb_s, bb_r, kb_s, kb_r, ak_s, ak_r, ab_s, ab_r,
     ax_s, ax_r, az_s, az_r, axg_s, axg_r, h_s, h_r, gt_s, gt_r, ob_s, ob_r, oz_s, oz_r) = scratch
    x = lax.axis_index("grp")
    r = lax.axis_index("row")
    c = lax.axis_index("col")
    b, k, h, z = r // 2, r % 2, c // 8, c % 8
    p = (b + h) % 2
    scale = 1.0 / 16384.0

    def dev(x_, b_, k_, h_, z_):
        return (x_, 2 * b_ + k_, 8 * h_ + z_)

    core_peer = dev(x, b, 1 - k, h, z)
    b_peer = dev(x, 1 - b, k, h, z)
    h_peer = dev(x, 1 - b, k, 1 - h, z)
    xp, xm, x2 = (x + 1) % 4, (x + 3) % 4, (x + 2) % 4
    xp_peer, xm_peer = dev(xp, b, k, h, z), dev(xm, b, k, h, z)
    zp_peer, zm_peer = dev(x, b, k, h, (z + 1) % 8), dev(x, b, k, h, (z + 7) % 8)

    def cp(src, dst, ss, rs, to):
        return pltpu.make_async_remote_copy(
            src_ref=src, dst_ref=dst, send_sem=ss, recv_sem=rs, device_id=to, device_id_type=MESH)

    sent = []

    def send(src, dst, ss, rs, to):
        d = cp(src, dst, ss, rs, to)
        d.start()
        sent.append(d)

    def got(dst, rs):
        cp(dst, dst, ld.at[9], rs, core_peer).wait_recv()

    l_g = pltpu.make_async_copy(grads.at[pl.ds(2 * p, 2), :, k], gsrc, ld.at[0])
    l_x = pltpu.make_async_copy(grads.at[pl.ds(2 * p, 2), x, k], xs.at[x], ld.at[1])
    rb_own = 2 * b + k
    l_b = pltpu.make_async_copy(gradb, bas.at[rb_own, pl.ds(pl.multiple_of(z * 256, 256), 256), :], ld.at[2])
    l_ab = pltpu.make_async_copy(actb, actv, ld.at[3])
    order = (2 * (1 - p) + 1 - k, 2 * (1 - p) + k, 2 * p + 1 - k, 2 * p + k)
    l_a = [pltpu.make_async_copy(acts.at[s], av.at[i], ld.at[4 + i]) for i, s in enumerate(order)]
    for d in [l_g, l_x, l_b, l_ab] + l_a:
        d.start()

    bar = pltpu.get_barrier_semaphore()

    def sig(to):
        pl.semaphore_signal(bar, inc=1, device_id=to, device_id_type=MESH)

    for to in (core_peer, b_peer, h_peer, xp_peer, xm_peer, dev(x2, b, k, h, z)):
        sig(to)

    @pl.loop(1, 8)
    def _(d):
        zt = (z + d) % 8
        sig(dev(x, b, k, h, zt))
        sig(dev(x, b, 1 - k, h, zt))

    pl.semaphore_wait(bar, 20)

    l_g.wait()
    for dx in (1, 3, 2):
        xt = (x + dx) % 4
        send(gsrc.at[:, xt], xs.at[x], xs_s.at[dx], xs_r.at[dx], dev(xt, b, k, h, z))

    def unit(rb, zs):
        return bas.at[rb, pl.ds(pl.multiple_of(zs * 256, 256), 256), :]

    def half(rb, zs, i):
        return bas.at[rb, pl.ds(pl.multiple_of(zs * 256 + 128 * i, 128), 128), :]

    rb_other = 2 * (1 - b) + k

    def b_send(zs):
        send(unit(rb_own, zs), unit(rb_own, zs), bb_s.at[zs], bb_r.at[zs], b_peer)

    l_b.wait()
    send(unit(rb_own, z), unit(rb_own, z), bz_s.at[0, 0], bz_r.at[0, 0], zp_peer)
    send(unit(rb_own, z), unit(rb_own, z), bz_s.at[1, 0], bz_r.at[1, 0], zm_peer)
    b_send(z)

    def ring(d):
        fwd, bwd = (z - d + 8) % 8, (z + d) % 8
        if d < 3:
            got(unit(rb_own, fwd), bz_r.at[0, d - 1])
            send(unit(rb_own, fwd), unit(rb_own, fwd), bz_s.at[0, d], bz_r.at[0, d], zp_peer)
            got(unit(rb_own, bwd), bz_r.at[1, d - 1])
            send(unit(rb_own, bwd), unit(rb_own, bwd), bz_s.at[1, d], bz_r.at[1, d], zm_peer)
            b_send(fwd)
            b_send(bwd)
        elif d == 3:
            got(unit(rb_own, fwd), bz_r.at[0, 2])
            send(half(rb_own, fwd, 0), half(rb_own, fwd, 0), bz_s.at[0, 3], bz_r.at[0, 3], zp_peer)
            got(unit(rb_own, bwd), bz_r.at[1, 2])
            send(half(rb_own, bwd, 1), half(rb_own, bwd, 1), bz_s.at[1, 3], bz_r.at[1, 3], zm_peer)
            b_send(fwd)
            b_send(bwd)
        else:
            got(half(rb_own, fwd, 0), bz_r.at[0, 3])
            got(half(rb_own, fwd, 1), bz_r.at[1, 3])
            b_send(fwd)
            send(bas.at[rb_own], bas.at[rb_own], kb_s.at[0], kb_r.at[0], core_peer)

    def a_part(i):
        l_a[i].wait()

        @pl.loop(0, 4)
        def _(m):
            rows = pl.ds(pl.multiple_of(m * 256, 256), 256)
            ap[i, rows, :] = jnp.dot(av[i, rows, :], actv[...], preferred_element_type=F32)

    l_ab.wait()
    a_part(0)
    send(ap.at[0], ar.at[0], ak_s.at[0], ak_r.at[0], core_peer)

    l_x.wait()
    for dx in (1, 3, 2):
        got(xs.at[(x + 4 - dx) % 4], xs_r.at[dx])
    lane = pl.ds(pl.multiple_of(z * 256, 256), 256)

    @pl.loop(1, 8)
    def _(d):
        zt = (z + d) % 8
        cp(xs.at[zt // 2, zt % 2], gq.at[x, :, lane], za_s.at[d], za_r.at[d], dev(x, b, k, h, zt)).start()

    gq[x, :, lane] = xs[z // 2, z % 2]

    ring(1)
    a_part(1)
    got(ar.at[0], ak_r.at[0])

    @pl.loop(0, 4)
    def _(m):
        rows = pl.ds(pl.multiple_of(m * 256, 256), 256)
        abs_[rows, :] = (ap[1, rows, :] + ar[0, rows, :]).astype(BF16)

    send(abs_, abr, ab_s, ab_r, b_peer)
    ring(2)
    a_part(2)
    send(ap.at[2], ar.at[1], ak_s.at[1], ak_r.at[1], core_peer)
    ring(3)
    a_part(3)
    ring(4)

    @pl.loop(1, 8)
    def _(d):
        zs = (z + 8 - d) % 8
        got(gq.at[x, :, pl.ds(pl.multiple_of(zs * 256, 256), 256)], za_r.at[d])

    def gh(q, i):
        return gq.at[q, pl.ds(64 * i, 64), :]

    for i, j, to in ((0, 0, xp_peer), (3, 1, xm_peer), (1, 1, xp_peer), (4, 0, xm_peer)):
        send(gh(x, j), gh(x, j), xg_s.at[i], xg_r.at[i], to)

    got(ar.at[1], ak_r.at[1])
    got(abr, ab_r)

    @pl.loop(0, 4)
    def _(m):
        rows = pl.ds(pl.multiple_of(m * 256, 256), 256)
        aown[m] = (ap[3, rows, :] + ar[1, rows, :] + abr[rows, :].astype(F32)).astype(BF16)

    for dx in (1, 3, 2):
        xt = (x + dx) % 4
        send(aown.at[xt], axs.at[x], ax_s.at[dx], ax_r.at[dx], dev(xt, b, k, h, z))
    axs[x] = aown[x]
    for dx in (1, 3, 2):
        got(axs.at[(x + 4 - dx) % 4], ax_r.at[dx])
    quarter = pl.ds(pl.multiple_of(x * 256, 256), 256)

    def az(e):
        return cp(axs.at[e], agat.at[z // 2, quarter, :], az_s.at[e], az_r.at[z // 2], dev(x, b, z % 2, h, 2 * e + k))

    for e in range(4):
        @pl.when(2 * e + k != z)
        def _():
            az(e).start()

        @pl.when(2 * e + k == z)
        def _():
            agat[z // 2, quarter, :] = axs[e]

    @pl.loop(0, 8)
    def _(zs):
        got(unit(rb_other, zs), bb_r.at[zs])

    send(bas.at[rb_other], bas.at[rb_other], kb_s.at[1], kb_r.at[1], core_peer)
    got(bas.at[2 * b + 1 - k], kb_r.at[0])
    got(bas.at[2 * (1 - b) + 1 - k], kb_r.at[1])

    def g_part(qi, q):
        for i, bb in enumerate((b, 1 - b)):
            for kk in range(2):
                rb = 2 * bb + kk
                part = jnp.dot(gq[q], bas[rb], preferred_element_type=F32)
                gp[q, rb] = part
                gs[q, rb] = part.astype(BF16)
            pair = pl.ds(2 * bb, 2)
            send(gs.at[q, pair], gr.at[q, pair], h_s.at[qi, i], h_r.at[qi, i], h_peer)

    g_part(0, x)
    got(gh(xm, 0), xg_r.at[0])
    send(gh(xm, 0), gh(xm, 0), xg_s.at[2], xg_r.at[2], xp_peer)
    got(gh(xp, 1), xg_r.at[3])
    send(gh(xp, 1), gh(xp, 1), xg_s.at[5], xg_r.at[5], xm_peer)

    for u in range(4):
        @pl.when(2 * u + k != z)
        def _():
            got(agat.at[u, quarter, :], az_r.at[u])

    def ah(q, j):
        return agat.at[pl.ds(2 * j, 2), pl.ds(pl.multiple_of(q * 256, 256), 256), :]

    for i, j, to in ((0, 0, xp_peer), (3, 1, xm_peer), (1, 1, xp_peer), (4, 0, xm_peer)):
        send(ah(x, j), ah(x, j), axg_s.at[i], axg_r.at[i], to)

    got(gh(xm, 1), xg_r.at[1])
    g_part(1, xm)
    got(gh(xp, 0), xg_r.at[4])
    g_part(2, xp)
    got(gh(x2, 0), xg_r.at[2])
    got(gh(x2, 1), xg_r.at[5])
    g_part(3, x2)

    got(ah(xm, 0), axg_r.at[0])
    send(ah(xm, 0), ah(xm, 0), axg_s.at[2], axg_r.at[2], xp_peer)
    got(ah(xp, 1), axg_r.at[3])
    send(ah(xp, 1), ah(xp, 1), axg_s.at[5], axg_r.at[5], xm_peer)

    def tok(q, kk):
        return pl.ds(pl.multiple_of(q * 256 + kk * 128, 128), 128)

    def g_done(qi, q):
        for i, bb in enumerate((1 - b, b)):
            pair = pl.ds(2 * bb, 2)
            got(gr.at[q, pair], h_r.at[qi, i])
            for kk in range(2):
                rb = 2 * bb + kk
                g = (gp[q, rb] + gr[q, rb].astype(F32)).astype(BF16)
                gt[rb, :, tok(q, k)] = g.T
        send(gt.at[:, :, tok(q, k)], gt.at[:, :, tok(q, k)], gt_s.at[qi], gt_r.at[qi], core_peer)

    for qi, q in enumerate((x, xm, xp, x2)):
        g_done(qi, q)
    for qi, q in enumerate((x, xm, xp, x2)):
        got(gt.at[:, :, tok(q, 1 - k)], gt_r.at[qi])

    got(ah(xm, 1), axg_r.at[1])
    got(ah(xp, 0), axg_r.at[4])
    got(ah(x2, 0), axg_r.at[2])
    got(ah(x2, 1), axg_r.at[5])

    def tile(rb, u):
        t = jnp.dot(gt[rb], agat[u], preferred_element_type=F32)
        return t * t * scale

    for u in range(4):
        for kk in range(2):
            ob[u, kk] = tile(2 * (1 - b) + kk, u).astype(BF16)
        send(ob.at[u], obr.at[u], ob_s.at[u], ob_r.at[u], b_peer)

    def oz(u, kk):
        return cp(zsnd.at[u, kk], fin.at[z], oz_s.at[u, kk], oz_r.at[z], dev(x, b, kk, h, 2 * u + k))

    def here(u, kk):
        return jnp.logical_and(2 * u + k == z, kk == k)

    for u in range(4):
        for kk in range(2):
            oacc[kk] = tile(2 * b + kk, u)
        got(obr.at[u], ob_r.at[u])
        for kk in range(2):
            v = (oacc[kk] + obr[u, kk].astype(F32)).astype(BF16)
            zsnd[u, kk] = v

            @pl.when(jnp.logical_not(here(u, kk)))
            def _():
                oz(u, kk).start()

            @pl.when(here(u, kk))
            def _():
                fin[z] = zsnd[u, kk]

    @pl.loop(0, 8)
    def _(zs):
        @pl.when(jnp.logical_not(jnp.logical_and(zs == z, z % 2 == k)))
        def _():
            got(fin.at[zs], oz_r.at[zs])

    total = fin[0].astype(F32)
    for i in range(1, 8):
        total = total + fin[i].astype(F32)
    out[...] = total

    for d in sent:
        d.wait_send()

    @pl.loop(1, 8)
    def _(d):
        zt = (z + d) % 8
        cp(xs.at[zt // 2, zt % 2], gq.at[x, :, lane], za_s.at[d], za_r.at[d], dev(x, b, k, h, zt)).wait_send()

    for e in range(4):
        @pl.when(2 * e + k != z)
        def _():
            az(e).wait_send()

    for u in range(4):
        for kk in range(2):
            @pl.when(jnp.logical_not(here(u, kk)))
            def _():
                oz(u, kk).wait_send()


def per_device(acts, grads, act_basis, grad_basis):
    grads = grads.reshape(4, 4, 2, 128, 256)
    V = pltpu.VMEM
    DMA = pltpu.SemaphoreType.DMA
    buffers = [
        V((2, 4, 128, 256), BF16), V((4, 2, 128, 256), BF16), V((4, 128, 2048), BF16), V((4, 2048, 256), BF16),
        V((4, 4, 128, 256), F32), V((4, 4, 128, 256), BF16), V((4, 4, 128, 256), BF16), V((4, 256, 1024), BF16),
        V((4, 1024, 1024), BF16), V((1024, 256), BF16), V((4, 1024, 256), F32), V((2, 1024, 256), F32),
        V((1024, 256), BF16), V((1024, 256), BF16), V((4, 256, 256), BF16), V((4, 256, 256), BF16),
        V((4, 1024, 256), BF16),
        V((4, 2, 256, 256), BF16), V((4, 2, 256, 256), BF16), V((2, 256, 256), F32), V((4, 2, 256, 256), BF16),
        V((8, 256, 256), BF16),
    ]
    sems = [DMA((10,)), DMA((4,)), DMA((4,)), DMA((8,)), DMA((8,)), DMA((6,)), DMA((6,)), DMA((2, 4)), DMA((2, 4)),
            DMA((8,)), DMA((8,)), DMA((2,)), DMA((2,)), DMA((2,)), DMA((2,)), DMA, DMA,
            DMA((4,)), DMA((4,)), DMA((4,)), DMA((4,)), DMA((6,)), DMA((6,)), DMA((4, 2)), DMA((4, 2)),
            DMA((4,)), DMA((4,)), DMA((4,)), DMA((4,)), DMA((4, 2)), DMA((8,))]
    hbm = pl.BlockSpec(memory_space=pl.ANY)
    return pl.pallas_call(
        kernel,
        out_shape=jax.ShapeDtypeStruct((256, 256), F32),
        in_specs=[hbm] * 4,
        out_specs=pl.BlockSpec(memory_space=pltpu.VMEM),
        scratch_shapes=buffers + sems,
        compiler_params=pltpu.CompilerParams(
            collective_id=0, has_side_effects=True, vmem_limit_bytes=56 * 2**20),
        cost_estimate=pl.CostEstimate(flops=6442450944, bytes_accessed=11534336, transcendentals=0),
    )(acts, grads, act_basis, grad_basis)


def solution(mesh):
    placed = (
        P("grp", None, "row"),
        P("grp", None, "col"),
        P("row", "col"),
        P("col", ("grp", "row")),
    )
    return jax.shard_map(
        per_device, mesh=mesh, in_specs=placed, out_specs=P(("grp", "row"), "col"), check_vma=False
    )
```

time: 524 us -> 133 us (0.25)
  waiting for transfers between devices: 361 us -> 0 us
  Pallas kernels: 0 us -> 131 us
  blocking collectives: 124 us -> 0 us
  matrix products: 22.8 us -> 0 us
  between operations: 13.1 us -> 0.01 us
    reduce_scatter x2 -> x0, waiting for transfers between devices: 314 us -> none  [the longest x1 290 us: per_device(): lax.psum_scatter(jnp.dot(grad_flat, panel, preferred_element_type=jnp.flo...]
    pallas_call x0 -> x1, Pallas kernels: none -> 131 us  [per_device(): pl.pallas_call(kernel, out_shape=jax.ShapeDtypeStruct((256, 256), F32), i...]
    psum x1 -> x0, blocking collectives: 111 us -> none  [per_device(): rotated_acts = lax.psum(act_terms, 'row').astype(jnp.bfloat16)]
    all_gather x1 -> x0, waiting for transfers between devices: 47.2 us -> none  [per_device(): lax.all_gather(shares.astype(jnp.bfloat16), 'col', axis=0, tiled=True)]
    dot_general x3 -> x0, matrix products: 22.8 us -> none  [the longest x1 8.06 us: per_device(): jnp.dot(grad_flat, panel, preferred_element_type=jnp.float32)]
    all_gather x1 -> x0, blocking collectives: 12.7 us -> none  [per_device(): panel = lax.all_gather(grad_basis, 'grp', axis=1, tiled=True)]
  transfers between devices with their start and end apart: 3 -> 0, of which waited for: 3 -> 0; matrix products, arithmetic and copies ran while one was open for 1% -> 0% of each run, Pallas kernels for 0% -> 0%
where the time goes in v1:
time: 133 us; the launch traced here: 132 us
  Pallas kernels  131 us (98%)
  local copies, waits for them, and re-layouts  1.67 us (1%)
    pallas_call x1, Pallas kernels, per_device(): pl.pallas_call(kernel, out_shape=jax.ShapeDtypeStruct((256, 256), F32), i...  131 us

profile of v1, /device:TPU:1, one launch (start us, length us, event | category | flops | bytes accessed | tf_op | source)
XLA Modules:
  0.0 132.4 jit_solution(12645819357489788213)
XLA Ops:
  0.0 130.8 %shard_map.46 = f32[256,256]{1,0:T(8,128)} custom-call(bf16[4,1024,1024]{2,1,0:T(8,128)(2,1)} %acts.1, bf16[4,4,2,128,256]{4,3,2,1,0:T(8,128)(2,1)} %bitcast.1, bf16[1024,256]{1,0:T(8,128)(2,1)} %actb.1, bf16[256,256]{1,0:T(8,128)(2,1)} %gradb.1), custom_call_target="tpu_custom_call" | custom-call | flops 6442450944 | bytes 11534336 | tf_op jit(solution)/shard_map/pallas_call | solution.py:349
  130.8 1.7 %copy.6 = f32[256,256]{1,0:T(8,128)} copy(f32[256,256]{1,0:T(8,128)} %shard_map.46) | data formatting | bytes 524288

commit v2 on v1

v2 whole, which is shorter than its diff:
```python
import jax
import jax.numpy as jnp
from jax import lax
from jax.experimental import pallas as pl
from jax.experimental.pallas import tpu as pltpu
from jax.sharding import PartitionSpec as P

MESH = pl.DeviceIdType.MESH
F32 = jnp.float32
BF16 = jnp.bfloat16


def kernel(acts, grads, actb, gradb, out, *scratch):
    (gsrc, xs, gq, bas, gp, gs, gr, gt, av, actv, ap, ar, abs_, abr, aown, axs, agat,
     ob, obr, oacc, zsnd, fin,
     ld, xs_s, xs_r, za_s, za_r, xg_s, xg_r, bz_s, bz_r, bb_s, bb_r, kb_s, kb_r, ak_s, ak_r, ab_s, ab_r,
     ax_s, ax_r, az_s, az_r, axg_s, axg_r, h_s, h_r, gt_s, gt_r, ob_s, ob_r, oz_s, oz_r) = scratch
    x = lax.axis_index("grp")
    r = lax.axis_index("row")
    c = lax.axis_index("col")
    b, k, h, z = r // 2, r % 2, c // 8, c % 8
    p = (b + h) % 2
    scale = 1.0 / 16384.0

    def dev(x_, b_, k_, h_, z_):
        return (x_, 2 * b_ + k_, 8 * h_ + z_)

    core_peer = dev(x, b, 1 - k, h, z)
    b_peer = dev(x, 1 - b, k, h, z)
    h_peer = dev(x, 1 - b, k, 1 - h, z)
    xp, xm, x2 = (x + 1) % 4, (x + 3) % 4, (x + 2) % 4
    xp_peer, xm_peer = dev(xp, b, k, h, z), dev(xm, b, k, h, z)
    zp_peer, zm_peer = dev(x, b, k, h, (z + 1) % 8), dev(x, b, k, h, (z + 7) % 8)

    def cp(src, dst, ss, rs, to):
        return pltpu.make_async_remote_copy(
            src_ref=src, dst_ref=dst, send_sem=ss, recv_sem=rs, device_id=to, device_id_type=MESH)

    sent = []

    def send(src, dst, ss, rs, to):
        d = cp(src, dst, ss, rs, to)
        d.start()
        sent.append(d)

    def got(dst, rs):
        cp(dst, dst, ld.at[9], rs, core_peer).wait_recv()

    l_g = pltpu.make_async_copy(grads.at[pl.ds(2 * p, 2), :, k], gsrc, ld.at[0])
    l_x = pltpu.make_async_copy(grads.at[pl.ds(2 * p, 2), x, k], xs.at[x], ld.at[1])
    rb_own = 2 * b + k
    l_b = pltpu.make_async_copy(gradb, bas.at[rb_own, pl.ds(pl.multiple_of(z * 256, 256), 256), :], ld.at[2])
    l_ab = pltpu.make_async_copy(actb, actv, ld.at[3])
    order = (2 * (1 - p) + 1 - k, 2 * (1 - p) + k, 2 * p + 1 - k, 2 * p + k)
    l_a = [pltpu.make_async_copy(acts.at[s], av.at[i], ld.at[4 + i]) for i, s in enumerate(order)]
    for d in [l_g, l_x, l_b, l_ab] + l_a:
        d.start()

    bar = pltpu.get_barrier_semaphore()

    def sig(to):
        pl.semaphore_signal(bar, inc=1, device_id=to, device_id_type=MESH)

    for to in (core_peer, b_peer, h_peer, xp_peer, xm_peer, dev(x2, b, k, h, z)):
        sig(to)

    @pl.loop(1, 8)
    def _(d):
        zt = (z + d) % 8
        sig(dev(x, b, k, h, zt))
        sig(dev(x, b, 1 - k, h, zt))

    pl.semaphore_wait(bar, 20)

    l_g.wait()
    for dx in (1, 3, 2):
        xt = (x + dx) % 4
        send(gsrc.at[:, xt], xs.at[x], xs_s.at[dx], xs_r.at[dx], dev(xt, b, k, h, z))

    def unit(rb, zs):
        return bas.at[rb, pl.ds(pl.multiple_of(zs * 256, 256), 256), :]

    def half(rb, zs, i):
        return bas.at[rb, pl.ds(pl.multiple_of(zs * 256 + 128 * i, 128), 128), :]

    rb_other = 2 * (1 - b) + k

    def b_send(zs):
        send(unit(rb_own, zs), unit(rb_own, zs), bb_s.at[zs], bb_r.at[zs], b_peer)

    def ring(d):
        fwd, bwd = (z - d + 8) % 8, (z + d) % 8
        if d == 0:
            l_b.wait()
            send(unit(rb_own, z), unit(rb_own, z), bz_s.at[0, 0], bz_r.at[0, 0], zp_peer)
            send(unit(rb_own, z), unit(rb_own, z), bz_s.at[1, 0], bz_r.at[1, 0], zm_peer)
        elif d < 3:
            got(unit(rb_own, fwd), bz_r.at[0, d - 1])
            send(unit(rb_own, fwd), unit(rb_own, fwd), bz_s.at[0, d], bz_r.at[0, d], zp_peer)
            got(unit(rb_own, bwd), bz_r.at[1, d - 1])
            send(unit(rb_own, bwd), unit(rb_own, bwd), bz_s.at[1, d], bz_r.at[1, d], zm_peer)
            b_send(fwd)
            b_send(bwd)
        elif d == 3:
            got(unit(rb_own, fwd), bz_r.at[0, 2])
            send(half(rb_own, fwd, 0), half(rb_own, fwd, 0), bz_s.at[0, 3], bz_r.at[0, 3], zp_peer)
            got(unit(rb_own, bwd), bz_r.at[1, 2])
            send(half(rb_own, bwd, 1), half(rb_own, bwd, 1), bz_s.at[1, 3], bz_r.at[1, 3], zm_peer)
            b_send(fwd)
            b_send(bwd)
        else:
            got(half(rb_own, fwd, 0), bz_r.at[0, 3])
            got(half(rb_own, fwd, 1), bz_r.at[1, 3])
            b_send(fwd)
            send(bas.at[rb_own], bas.at[rb_own], kb_s.at[0], kb_r.at[0], core_peer)

    lane = pl.ds(pl.multiple_of(z * 256, 256), 256)

    def za_copy(e, j):
        zt = 2 * e + j
        return cp(xs.at[e, j], gq.at[x, :, lane], za_s.at[zt], za_r.at[(zt + 8 - z) % 8], dev(x, b, k, h, zt))

    def za(e):
        for j in range(2):
            @pl.when(2 * e + j != z)
            def _():
                za_copy(e, j).start()

            @pl.when(2 * e + j == z)
            def _():
                gq[x, :, lane] = xs[e, j]

    pieces = (0, 1, 7, 2, 6, 3, 5, 4)

    def gpiece(q, d):
        zs = (z + 8 - d) % 8
        return gq.at[q, :, pl.ds(pl.multiple_of(zs * 256, 256), 256)]

    def xg(i):
        d = pieces[i]
        if d:
            got(gpiece(x, d), za_r.at[d])
        send(gpiece(x, d), gpiece(x, d), xg_s.at[0, d], xg_r.at[0, d], xp_peer)
        send(gpiece(x, d), gpiece(x, d), xg_s.at[1, d], xg_r.at[1, d], xm_peer)

    def xg_forward(i):
        d = pieces[i]
        if i % 2 == 0:
            got(gpiece(xm, d), xg_r.at[0, d])
            send(gpiece(xm, d), gpiece(xm, d), xg_s.at[2, d], xg_r.at[2, d], xp_peer)
        else:
            got(gpiece(xp, d), xg_r.at[1, d])
            send(gpiece(xp, d), gpiece(xp, d), xg_s.at[2, d], xg_r.at[2, d], xm_peer)

    def xg_rest(side):
        for i, d in enumerate(pieces):
            if side == 2 or i % 2 != side:
                got(gpiece((xm, xp, x2)[side], d), xg_r.at[side, d])

    def a_part(i):
        if i == 0:
            l_ab.wait()
        l_a[i].wait()

        @pl.loop(0, 4)
        def _(m):
            rows = pl.ds(pl.multiple_of(m * 256, 256), 256)
            ap[i, rows, :] = jnp.dot(av[i, rows, :], actv[...], preferred_element_type=F32)

        if i % 2 == 0:
            send(ap.at[i], ar.at[i // 2], ak_s.at[i // 2], ak_r.at[i // 2], core_peer)

    def a_to_b():
        got(ar.at[0], ak_r.at[0])

        @pl.loop(0, 4)
        def _(m):
            rows = pl.ds(pl.multiple_of(m * 256, 256), 256)
            abs_[rows, :] = (ap[1, rows, :] + ar[0, rows, :]).astype(BF16)

        send(abs_, abr, ab_s, ab_r, b_peer)

    def a_sum():
        got(ar.at[1], ak_r.at[1])
        got(abr, ab_r)

        @pl.loop(0, 4)
        def _(m):
            rows = pl.ds(pl.multiple_of(m * 256, 256), 256)
            aown[m] = (ap[3, rows, :] + ar[1, rows, :] + abr[rows, :].astype(F32)).astype(BF16)

        for dx in (1, 3, 2):
            xt = (x + dx) % 4
            send(aown.at[xt], axs.at[x], ax_s.at[dx], ax_r.at[dx], dev(xt, b, k, h, z))
        axs[x] = aown[x]

    quarter = pl.ds(pl.multiple_of(x * 256, 256), 256)

    def az_copy(e):
        return cp(axs.at[e], agat.at[z // 2, quarter, :], az_s.at[e], az_r.at[z // 2], dev(x, b, z % 2, h, 2 * e + k))

    def az(e):
        @pl.when(2 * e + k != z)
        def _():
            az_copy(e).start()

        @pl.when(2 * e + k == z)
        def _():
            agat[z // 2, quarter, :] = axs[e]

    def apiece(q, u):
        return agat.at[u, pl.ds(pl.multiple_of(q * 256, 256), 256), :]

    def axg(u):
        @pl.when(2 * u + k != z)
        def _():
            got(agat.at[u, quarter, :], az_r.at[u])

        send(apiece(x, u), apiece(x, u), axg_s.at[0, u], axg_r.at[0, u], xp_peer)
        send(apiece(x, u), apiece(x, u), axg_s.at[1, u], axg_r.at[1, u], xm_peer)

    def axg_forward(u):
        if u % 2 == 0:
            got(apiece(xm, u), axg_r.at[0, u])
            send(apiece(xm, u), apiece(xm, u), axg_s.at[2, u], axg_r.at[2, u], xp_peer)
        else:
            got(apiece(xp, u), axg_r.at[1, u])
            send(apiece(xp, u), apiece(xp, u), axg_s.at[2, u], axg_r.at[2, u], xm_peer)

    def axg_rest(u):
        if u % 2 == 0:
            got(apiece(xp, u), axg_r.at[1, u])
        else:
            got(apiece(xm, u), axg_r.at[0, u])
        got(apiece(x2, u), axg_r.at[2, u])

    quarters = (x, xm, xp, x2)

    def g_part(qi, i):
        q, bb = quarters[qi], (b, 1 - b)[i]
        for kk in range(2):
            rb = 2 * bb + kk
            part = jnp.dot(gq[q], bas[rb], preferred_element_type=F32)
            gp[q, rb] = part
            gs[q, rb] = part.astype(BF16)
        pair = pl.ds(2 * bb, 2)
        send(gs.at[q, pair], gr.at[q, pair], h_s.at[qi, i], h_r.at[qi, i], h_peer)

    def tok(q, kk):
        return pl.ds(pl.multiple_of(q * 256 + kk * 128, 128), 128)

    def g_done(qi, i):
        q, bb = quarters[qi], (1 - b, b)[i]
        pair = pl.ds(2 * bb, 2)
        got(gr.at[q, pair], h_r.at[qi, i])
        for kk in range(2):
            rb = 2 * bb + kk
            g = (gp[q, rb] + gr[q, rb].astype(F32)).astype(BF16)
            gt[rb, :, tok(q, k)] = g.T
        mine = gt.at[pair, :, tok(q, k)]
        send(mine, mine, gt_s.at[qi, i], gt_r.at[qi, i], core_peer)

    def g_shared(i):
        pair = pl.ds(2 * (1 - b, b)[i], 2)
        for qi in range(4):
            got(gt.at[pair, :, tok(quarters[qi], 1 - k)], gt_r.at[qi, i])

    def tile(rb, u):
        t = jnp.dot(gt[rb], agat[u], preferred_element_type=F32)
        return t * t * scale

    def ob_send(u):
        for kk in range(2):
            ob[u, kk] = tile(2 * (1 - b) + kk, u).astype(BF16)
        send(ob.at[u], obr.at[u], ob_s.at[u], ob_r.at[u], b_peer)

    def oz_copy(u, kk):
        return cp(zsnd.at[u, kk], fin.at[z], oz_s.at[u, kk], oz_r.at[z], dev(x, b, kk, h, 2 * u + k))

    def here(u, kk):
        return jnp.logical_and(2 * u + k == z, kk == k)

    def oz(u):
        for kk in range(2):
            oacc[kk] = tile(2 * b + kk, u)
        got(obr.at[u], ob_r.at[u])
        for kk in range(2):
            zsnd[u, kk] = (oacc[kk] + obr[u, kk].astype(F32)).astype(BF16)

            @pl.when(jnp.logical_not(here(u, kk)))
            def _():
                oz_copy(u, kk).start()

            @pl.when(here(u, kk))
            def _():
                fin[z] = zsnd[u, kk]

    ring(0)
    l_x.wait()
    za(x)
    a_part(0)
    a_part(1)
    a_to_b()
    got(xs.at[xm], xs_r.at[1])
    za(xm)
    got(xs.at[xp], xs_r.at[3])
    za(xp)
    ring(1)
    got(xs.at[x2], xs_r.at[2])
    za(x2)
    b_send(z)
    xg(0)
    xg(1)
    ring(2)
    xg(2)
    a_part(2)
    xg_forward(0)
    xg(3)
    xg_forward(1)
    a_part(3)
    ring(3)
    xg(4)
    xg_forward(2)
    a_sum()
    xg(5)
    xg_forward(3)
    ring(4)
    xg(6)
    xg_forward(4)
    xg(7)
    xg_forward(5)
    az(x)
    got(axs.at[xm], ax_r.at[1])
    az(xm)
    got(axs.at[xp], ax_r.at[3])
    az(xp)
    xg_forward(6)
    got(axs.at[x2], ax_r.at[2])
    az(x2)
    xg_forward(7)
    got(bas.at[2 * b + 1 - k], kb_r.at[0])
    g_part(0, 0)
    xg_rest(0)
    g_part(1, 0)
    xg_rest(1)
    g_part(2, 0)
    xg_rest(2)
    g_part(3, 0)
    axg(0)
    axg(1)
    axg_forward(0)

    @pl.loop(0, 8)
    def _(zs):
        got(unit(rb_other, zs), bb_r.at[zs])

    send(bas.at[rb_other], bas.at[rb_other], kb_s.at[1], kb_r.at[1], core_peer)
    axg(2)
    axg_forward(1)
    got(bas.at[2 * (1 - b) + 1 - k], kb_r.at[1])
    for qi in range(4):
        g_part(qi, 1)
    axg(3)
    axg_forward(2)
    for qi in range(4):
        g_done(qi, 0)
    axg_forward(3)
    g_shared(0)
    axg_rest(0)
    ob_send(0)
    axg_rest(1)
    ob_send(1)
    for qi in range(4):
        g_done(qi, 1)
    axg_rest(2)
    ob_send(2)
    axg_rest(3)
    ob_send(3)
    g_shared(1)
    for u in range(4):
        oz(u)

    @pl.loop(0, 8)
    def _(zs):
        @pl.when(jnp.logical_not(jnp.logical_and(zs == z, z % 2 == k)))
        def _():
            got(fin.at[zs], oz_r.at[zs])

    total = fin[0].astype(F32)
    for i in range(1, 8):
        total = total + fin[i].astype(F32)
    out[...] = total

    for d in sent:
        d.wait_send()

    for e in range(4):
        for j in range(2):
            @pl.when(2 * e + j != z)
            def _():
                za_copy(e, j).wait_send()

        @pl.when(2 * e + k != z)
        def _():
            az_copy(e).wait_send()

    for u in range(4):
        for kk in range(2):
            @pl.when(jnp.logical_not(here(u, kk)))
            def _():
                oz_copy(u, kk).wait_send()


def per_device(acts, grads, act_basis, grad_basis):
    grads = grads.reshape(4, 4, 2, 128, 256)
    V = pltpu.VMEM
    DMA = pltpu.SemaphoreType.DMA
    buffers = [
        V((2, 4, 128, 256), BF16), V((4, 2, 128, 256), BF16), V((4, 128, 2048), BF16), V((4, 2048, 256), BF16),
        V((4, 4, 128, 256), F32), V((4, 4, 128, 256), BF16), V((4, 4, 128, 256), BF16), V((4, 256, 1024), BF16),
        V((4, 1024, 1024), BF16), V((1024, 256), BF16), V((4, 1024, 256), F32), V((2, 1024, 256), F32),
        V((1024, 256), BF16), V((1024, 256), BF16), V((4, 256, 256), BF16), V((4, 256, 256), BF16),
        V((4, 1024, 256), BF16),
        V((4, 2, 256, 256), BF16), V((4, 2, 256, 256), BF16), V((2, 256, 256), F32), V((4, 2, 256, 256), BF16),
        V((8, 256, 256), BF16),
    ]
    sems = [DMA((10,)), DMA((4,)), DMA((4,)), DMA((8,)), DMA((8,)), DMA((3, 8)), DMA((3, 8)), DMA((2, 4)), DMA((2, 4)),
            DMA((8,)), DMA((8,)), DMA((2,)), DMA((2,)), DMA((2,)), DMA((2,)), DMA, DMA,
            DMA((4,)), DMA((4,)), DMA((4,)), DMA((4,)), DMA((3, 4)), DMA((3, 4)), DMA((4, 2)), DMA((4, 2)),
            DMA((4, 2)), DMA((4, 2)), DMA((4,)), DMA((4,)), DMA((4, 2)), DMA((8,))]
    hbm = pl.BlockSpec(memory_space=pl.ANY)
    return pl.pallas_call(
        kernel,
        out_shape=jax.ShapeDtypeStruct((256, 256), F32),
        in_specs=[hbm] * 4,
        out_specs=pl.BlockSpec(memory_space=pltpu.VMEM),
        scratch_shapes=buffers + sems,
        compiler_params=pltpu.CompilerParams(
            collective_id=0, has_side_effects=True, vmem_limit_bytes=56 * 2**20),
        cost_estimate=pl.CostEstimate(flops=6442450944, bytes_accessed=11534336, transcendentals=0),
    )(acts, grads, act_basis, grad_basis)


def solution(mesh):
    placed = (
        P("grp", None, "row"),
        P("grp", None, "col"),
        P("row", "col"),
        P("col", ("grp", "row")),
    )
    return jax.shard_map(
        per_device, mesh=mesh, in_specs=placed, out_specs=P(("grp", "row"), "col"), check_vma=False
    )
```

time: 133 us -> 114 us (0.86)
  Pallas kernels: 131 us -> 112 us
    pallas_call x1, Pallas kernels: 131 us -> 112 us  [per_device(): pl.pallas_call(kernel, out_shape=jax.ShapeDtypeStruct((256, 256), F32), i...]
where the time goes in v2:
time: 114 us
  Pallas kernels  112 us (98%)
  local copies, waits for them, and re-layouts  1.67 us (1%)
    pallas_call x1, Pallas kernels, per_device(): pl.pallas_call(kernel, out_shape=jax.ShapeDtypeStruct((256, 256), F32), i...  112 us

profile of v2, /device:TPU:1, one launch (start us, length us, event | category | flops | bytes accessed | tf_op | source)
XLA Modules:
  0.0 114.1 jit_solution(10521330338428609245)
XLA Ops:
  0.0 112.4 %shard_map.46 = f32[256,256]{1,0:T(8,128)} custom-call(bf16[4,1024,1024]{2,1,0:T(8,128)(2,1)} %acts.1, bf16[4,4,2,128,256]{4,3,2,1,0:T(8,128)(2,1)} %bitcast.1, bf16[1024,256]{1,0:T(8,128)(2,1)} %actb.1, bf16[256,256]{1,0:T(8,128)(2,1)} %gradb.1), custom_call_target="tpu_custom_call" | custom-call | flops 6442450944 | bytes 11534336 | tf_op jit(solution)/shard_map/pallas_call | solution.py:432
  112.4 1.7 %copy.6 = f32[256,256]{1,0:T(8,128)} copy(f32[256,256]{1,0:T(8,128)} %shard_map.46) | data formatting | bytes 524288

commit v3 on v2

--- a/solution.py
+++ b/solution.py
@@ -12,9 +12,9 @@
 
 def kernel(acts, grads, actb, gradb, out, *scratch):
     (gsrc, xs, gq, bas, gp, gs, gr, gt, av, actv, ap, ar, abs_, abr, aown, axs, agat,
-     ob, obr, oacc, zsnd, fin,
+     ob, obr, oacc, zsnd, fin, mrg,
      ld, xs_s, xs_r, za_s, za_r, xg_s, xg_r, bz_s, bz_r, bb_s, bb_r, kb_s, kb_r, ak_s, ak_r, ab_s, ab_r,
-     ax_s, ax_r, az_s, az_r, axg_s, axg_r, h_s, h_r, gt_s, gt_r, ob_s, ob_r, oz_s, oz_r) = scratch
+     ax_s, ax_r, az_s, az_r, axg_s, axg_r, h_s, h_r, gt_s, gt_r, ob_s, ob_r, oz_s, oz_r, mg_r) = scratch
     x = lax.axis_index("grp")
     r = lax.axis_index("row")
     c = lax.axis_index("col")
@@ -208,31 +208,35 @@
         def _():
             agat[z // 2, quarter, :] = axs[e]
 
-    def apiece(q, u):
-        return agat.at[u, pl.ds(pl.multiple_of(q * 256, 256), 256), :]
-
-    def axg(u):
-        @pl.when(2 * u + k != z)
+    even = 1 - (z + k) % 2
+    far = (3 + even, 5 - 3 * even, 1 + 5 * even, 7 - 7 * even)
+    units = tuple((z + f) % 8 // 2 for f in far)
+
+    def apiece(q, i):
+        return agat.at[units[i], pl.ds(pl.multiple_of(q * 256, 256), 256), :]
+
+    def axg(i):
+        @pl.when(2 * units[i] + k != z)
         def _():
-            got(agat.at[u, quarter, :], az_r.at[u])
-
-        send(apiece(x, u), apiece(x, u), axg_s.at[0, u], axg_r.at[0, u], xp_peer)
-        send(apiece(x, u), apiece(x, u), axg_s.at[1, u], axg_r.at[1, u], xm_peer)
-
-    def axg_forward(u):
-        if u % 2 == 0:
-            got(apiece(xm, u), axg_r.at[0, u])
-            send(apiece(xm, u), apiece(xm, u), axg_s.at[2, u], axg_r.at[2, u], xp_peer)
+            got(apiece(x, i), az_r.at[units[i]])
+
+        send(apiece(x, i), apiece(x, i), axg_s.at[0, i], axg_r.at[0, i], xp_peer)
+        send(apiece(x, i), apiece(x, i), axg_s.at[1, i], axg_r.at[1, i], xm_peer)
+
+    def axg_forward(i):
+        if i % 2 == 0:
+            got(apiece(xm, i), axg_r.at[0, i])
+            send(apiece(xm, i), apiece(xm, i), axg_s.at[2, i], axg_r.at[2, i], xp_peer)
         else:
-            got(apiece(xp, u), axg_r.at[1, u])
-            send(apiece(xp, u), apiece(xp, u), axg_s.at[2, u], axg_r.at[2, u], xm_peer)
-
-    def axg_rest(u):
-        if u % 2 == 0:
-            got(apiece(xp, u), axg_r.at[1, u])
+            got(apiece(xp, i), axg_r.at[1, i])
+            send(apiece(xp, i), apiece(xp, i), axg_s.at[2, i], axg_r.at[2, i], xm_peer)
+
+    def axg_rest(i):
+        if i % 2 == 0:
+            got(apiece(xp, i), axg_r.at[1, i])
         else:
-            got(apiece(xm, u), axg_r.at[0, u])
-        got(apiece(x2, u), axg_r.at[2, u])
+            got(apiece(xm, i), axg_r.at[0, i])
+        got(apiece(x2, i), axg_r.at[2, i])
 
     quarters = (x, xm, xp, x2)
 
@@ -269,31 +273,52 @@
         t = jnp.dot(gt[rb], agat[u], preferred_element_type=F32)
         return t * t * scale
 
-    def ob_send(u):
+    def ob_send(i):
         for kk in range(2):
-            ob[u, kk] = tile(2 * (1 - b) + kk, u).astype(BF16)
-        send(ob.at[u], obr.at[u], ob_s.at[u], ob_r.at[u], b_peer)
-
-    def oz_copy(u, kk):
-        return cp(zsnd.at[u, kk], fin.at[z], oz_s.at[u, kk], oz_r.at[z], dev(x, b, kk, h, 2 * u + k))
-
-    def here(u, kk):
-        return jnp.logical_and(2 * u + k == z, kk == k)
-
-    def oz(u):
+            ob[i, kk] = tile(2 * (1 - b) + kk, units[i]).astype(BF16)
+            send(ob.at[i, kk], obr.at[i, kk], ob_s.at[i, kk], ob_r.at[i, kk], b_peer)
+
+    def oz_copy(i, kk):
+        return cp(zsnd.at[i, kk], fin.at[z], oz_s.at[i, kk], oz_r.at[z], dev(x, b, kk, h, (z + far[i]) % 8))
+
+    def merge_copy(i, kk):
+        return cp(zsnd.at[i, kk], mrg.at[i, kk], oz_s.at[i, kk], mg_r.at[i, kk], (zp_peer, zm_peer)[i])
+
+    def here(i, kk):
+        return jnp.logical_and(even == 1, kk == k)
+
+    def oz(i):
         for kk in range(2):
-            oacc[kk] = tile(2 * b + kk, u)
-        got(obr.at[u], ob_r.at[u])
-        for kk in range(2):
-            zsnd[u, kk] = (oacc[kk] + obr[u, kk].astype(F32)).astype(BF16)
-
-            @pl.when(jnp.logical_not(here(u, kk)))
-            def _():
-                oz_copy(u, kk).start()
-
-            @pl.when(here(u, kk))
-            def _():
-                fin[z] = zsnd[u, kk]
+            oacc[...] = tile(2 * b + kk, units[i])
+            got(obr.at[i, kk], ob_r.at[i, kk])
+            v = oacc[...] + obr[i, kk].astype(F32)
+            zsnd[i, kk] = v.astype(BF16)
+            if i in (1, 2):
+                oacc[...] = v
+
+                @pl.when(even == 1)
+                def _():
+                    got(mrg.at[i - 1, kk], mg_r.at[i - 1, kk])
+                    zsnd[i, kk] = (oacc[...] + mrg[i - 1, kk].astype(F32)).astype(BF16)
+
+            if i < 2:
+                @pl.when(even == 0)
+                def _():
+                    merge_copy(i, kk).start()
+
+                @pl.when(even == 1)
+                def _():
+                    oz_copy(i, kk).start()
+            elif i == 2:
+                oz_copy(i, kk).start()
+            else:
+                @pl.when(jnp.logical_not(here(i, kk)))
+                def _():
+                    oz_copy(i, kk).start()
+
+                @pl.when(here(i, kk))
+                def _():
+                    fin[z] = zsnd[i, kk]
 
     ring(0)
     l_x.wait()
@@ -361,13 +386,13 @@
     for qi in range(4):
         g_part(qi, 1)
     axg(3)
-    axg_forward(2)
     for qi in range(4):
         g_done(qi, 0)
-    axg_forward(3)
     g_shared(0)
+    axg_forward(2)
     axg_rest(0)
     ob_send(0)
+    axg_forward(3)
     axg_rest(1)
     ob_send(1)
     for qi in range(4):
@@ -380,15 +405,17 @@
     for u in range(4):
         oz(u)
 
-    @pl.loop(0, 8)
-    def _(zs):
-        @pl.when(jnp.logical_not(jnp.logical_and(zs == z, z % 2 == k)))
-        def _():
+    total = None
+    for off in (4, 2, 6, 1, 7, 0):
+        zs = (z + off) % 8
+        if off:
             got(fin.at[zs], oz_r.at[zs])
-
-    total = fin[0].astype(F32)
-    for i in range(1, 8):
-        total = total + fin[i].astype(F32)
+        else:
+            @pl.when(even == 0)
+            def _():
+                got(fin.at[z], oz_r.at[z])
+        part = fin[zs].astype(F32)
+        total = part if total is None else total + part
     out[...] = total
 
     for d in sent:
@@ -404,11 +431,14 @@
         def _():
             az_copy(e).wait_send()
 
-    for u in range(4):
+    for i in range(4):
         for kk in range(2):
-            @pl.when(jnp.logical_not(here(u, kk)))
-            def _():
-                oz_copy(u, kk).wait_send()
+            if i < 3:
+                oz_copy(i, kk).wait_send()
+            else:
+                @pl.when(jnp.logical_not(here(i, kk)))
+                def _():
+                    oz_copy(i, kk).wait_send()
 
 
 def per_device(acts, grads, act_basis, grad_basis):
@@ -421,13 +451,13 @@
         V((4, 1024, 1024), BF16), V((1024, 256), BF16), V((4, 1024, 256), F32), V((2, 1024, 256), F32),
         V((1024, 256), BF16), V((1024, 256), BF16), V((4, 256, 256), BF16), V((4, 256, 256), BF16),
         V((4, 1024, 256), BF16),
-        V((4, 2, 256, 256), BF16), V((4, 2, 256, 256), BF16), V((2, 256, 256), F32), V((4, 2, 256, 256), BF16),
-        V((8, 256, 256), BF16),
+        V((4, 2, 256, 256), BF16), V((4, 2, 256, 256), BF16), V((256, 256), F32), V((4, 2, 256, 256), BF16),
+        V((8, 256, 256), BF16), V((2, 2, 256, 256), BF16),
     ]
     sems = [DMA((10,)), DMA((4,)), DMA((4,)), DMA((8,)), DMA((8,)), DMA((3, 8)), DMA((3, 8)), DMA((2, 4)), DMA((2, 4)),
             DMA((8,)), DMA((8,)), DMA((2,)), DMA((2,)), DMA((2,)), DMA((2,)), DMA, DMA,
             DMA((4,)), DMA((4,)), DMA((4,)), DMA((4,)), DMA((3, 4)), DMA((3, 4)), DMA((4, 2)), DMA((4, 2)),
-            DMA((4, 2)), DMA((4, 2)), DMA((4,)), DMA((4,)), DMA((4, 2)), DMA((8,))]
+            DMA((4, 2)), DMA((4, 2)), DMA((4, 2)), DMA((4, 2)), DMA((4, 2)), DMA((8,)), DMA((2, 2))]
     hbm = pl.BlockSpec(memory_space=pl.ANY)
     return pl.pallas_call(
         kernel,

time: 114 us -> 106 us (0.930); the launches traced: 114 us -> 105 us
  Pallas kernels: 112 us -> 103 us
    pallas_call x1, Pallas kernels: 112 us -> 103 us  [per_device(): pl.pallas_call(kernel, out_shape=jax.ShapeDtypeStruct((256, 256), F32), i...]
where the time goes in v3:
time: 106 us; the launch traced here: 105 us
  Pallas kernels  103 us (97%)
  local copies, waits for them, and re-layouts  1.67 us (2%)
    pallas_call x1, Pallas kernels, per_device(): pl.pallas_call(kernel, out_shape=jax.ShapeDtypeStruct((256, 256), F32), i...  103 us

profile of v3, /device:TPU:1, one launch (start us, length us, event | category | flops | bytes accessed | tf_op | source)
XLA Modules:
  0.0 104.6 jit_solution(17459848737558600053)
XLA Ops:
  0.0 102.9 %shard_map.46 = f32[256,256]{1,0:T(8,128)} custom-call(bf16[4,1024,1024]{2,1,0:T(8,128)(2,1)} %acts.1, bf16[4,4,2,128,256]{4,3,2,1,0:T(8,128)(2,1)} %bitcast.1, bf16[1024,256]{1,0:T(8,128)(2,1)} %actb.1, bf16[256,256]{1,0:T(8,128)(2,1)} %gradb.1), custom_call_target="tpu_custom_call" | custom-call | flops 6442450944 | bytes 11534336 | tf_op jit(solution)/shard_map/pallas_call | solution.py:462
  103.0 1.7 %copy.6 = f32[256,256]{1,0:T(8,128)} copy(f32[256,256]{1,0:T(8,128)} %shard_map.46) | data formatting | bytes 524288

commit v4 on v3

--- a/solution.py
+++ b/solution.py
@@ -325,12 +325,12 @@
     za(x)
     a_part(0)
     a_part(1)
+    ring(1)
     a_to_b()
     got(xs.at[xm], xs_r.at[1])
     za(xm)
     got(xs.at[xp], xs_r.at[3])
     za(xp)
-    ring(1)
     got(xs.at[x2], xs_r.at[2])
     za(x2)
     b_send(z)
@@ -365,14 +365,14 @@
     xg_forward(7)
     got(bas.at[2 * b + 1 - k], kb_r.at[0])
     g_part(0, 0)
+    axg(0)
     xg_rest(0)
     g_part(1, 0)
+    axg(1)
     xg_rest(1)
     g_part(2, 0)
     xg_rest(2)
     g_part(3, 0)
-    axg(0)
-    axg(1)
     axg_forward(0)
 
     @pl.loop(0, 8)

time: 106 us -> 104 us (0.981)
    pallas_call x1, Pallas kernels: 103 us -> 102 us  [per_device(): pl.pallas_call(kernel, out_shape=jax.ShapeDtypeStruct((256, 256), F32), i...]
where the time goes in v4:
time: 104 us; the launch traced here: 103 us
  Pallas kernels  102 us (98%)
  local copies, waits for them, and re-layouts  1.67 us (2%)
    pallas_call x1, Pallas kernels, per_device(): pl.pallas_call(kernel, out_shape=jax.ShapeDtypeStruct((256, 256), F32), i...  102 us

profile of v4, /device:TPU:1, one launch (start us, length us, event | category | flops | bytes accessed | tf_op | source)
XLA Modules:
  0.0 103.4 jit_solution(7745600083724791863)
XLA Ops:
  0.0 101.7 %shard_map.46 = f32[256,256]{1,0:T(8,128)} custom-call(bf16[4,1024,1024]{2,1,0:T(8,128)(2,1)} %acts.1, bf16[4,4,2,128,256]{4,3,2,1,0:T(8,128)(2,1)} %bitcast.1, bf16[1024,256]{1,0:T(8,128)(2,1)} %actb.1, bf16[256,256]{1,0:T(8,128)(2,1)} %gradb.1), custom_call_target="tpu_custom_call" | custom-call | flops 6442450944 | bytes 11534336 | tf_op jit(solution)/shard_map/pallas_call | solution.py:462
  101.8 1.7 %copy.6 = f32[256,256]{1,0:T(8,128)} copy(f32[256,256]{1,0:T(8,128)} %shard_map.46) | data formatting | bytes 524288

commit v5 on v4

--- a/solution.py
+++ b/solution.py
@@ -345,8 +345,8 @@
     a_part(3)
     ring(3)
     xg(4)
+    a_sum()
     xg_forward(2)
-    a_sum()
     xg(5)
     xg_forward(3)
     ring(4)
@@ -405,8 +405,7 @@
     for u in range(4):
         oz(u)
 
-    total = None
-    for off in (4, 2, 6, 1, 7, 0):
+    for i, off in enumerate((4, 2, 6, 1, 7, 0)):
         zs = (z + off) % 8
         if off:
             got(fin.at[zs], oz_r.at[zs])
@@ -414,9 +413,7 @@
             @pl.when(even == 0)
             def _():
                 got(fin.at[z], oz_r.at[z])
-        part = fin[zs].astype(F32)
-        total = part if total is None else total + part
-    out[...] = total
+        out[i] = fin[zs]
 
     for d in sent:
         d.wait_send()
@@ -459,9 +456,9 @@
             DMA((4,)), DMA((4,)), DMA((4,)), DMA((4,)), DMA((3, 4)), DMA((3, 4)), DMA((4, 2)), DMA((4, 2)),
             DMA((4, 2)), DMA((4, 2)), DMA((4, 2)), DMA((4, 2)), DMA((4, 2)), DMA((8,)), DMA((2, 2))]
     hbm = pl.BlockSpec(memory_space=pl.ANY)
-    return pl.pallas_call(
+    parts = pl.pallas_call(
         kernel,
-        out_shape=jax.ShapeDtypeStruct((256, 256), F32),
+        out_shape=jax.ShapeDtypeStruct((6, 256, 256), BF16),
         in_specs=[hbm] * 4,
         out_specs=pl.BlockSpec(memory_space=pltpu.VMEM),
         scratch_shapes=buffers + sems,
@@ -469,6 +466,7 @@
             collective_id=0, has_side_effects=True, vmem_limit_bytes=56 * 2**20),
         cost_estimate=pl.CostEstimate(flops=6442450944, bytes_accessed=11534336, transcendentals=0),
     )(acts, grads, act_basis, grad_basis)
+    return jnp.sum(parts.astype(F32), axis=0)
 
 
 def solution(mesh):

time: 104 us -> 104 us (level)
  other arithmetic: 0 us -> 1.96 us
  local copies, waits for them, and re-layouts: 1.67 us -> 0 us
    reduce_sum x0 -> x1, other arithmetic: none -> 1.96 us  [per_device(): return jnp.sum(parts.astype(F32), axis=0)]
    unnamed x1 -> x0, local copies, waits for them, and re-layouts: 1.67 us -> none
where the time goes in v5:
time: 104 us
  Pallas kernels  102 us (98%)
  other arithmetic  1.96 us (2%)
    pallas_call x1, Pallas kernels, per_device(): pl.pallas_call(kernel, out_shape=jax.ShapeDtypeStruct((6, 256, 256), BF16...  102 us

profile of v5, /device:TPU:1, one launch (start us, length us, event | category | flops | bytes accessed | tf_op | source)
XLA Modules:
  0.0 103.9 jit_solution(11986673314133106953)
XLA Ops:
  0.0 102.0 %shard_map.46 = bf16[6,256,256]{2,1,0:T(8,128)(2,1)} custom-call(bf16[4,1024,1024]{2,1,0:T(8,128)(2,1)} %acts.1, bf16[4,4,2,128,256]{4,3,2,1,0:T(8,128)(2,1)} %bitcast.1, bf16[1024,256]{1,0:T(8,128)(2,1)} %actb.1, bf16[256,256]{1,0:T(8,128)(2,1)} %gradb.1), custom_call_target="tpu_custom_call" | custom-call | flops 6442450944 | bytes 11534336 | tf_op jit(solution)/shard_map/pallas_call | solution.py:459
  102.0 2.0 %convert_reduce_fusion = f32[256,256]{1,0:T(8,128)} fusion(bf16[6,256,256]{2,1,0:T(8,128)(2,1)} %shard_map.46), kind=kLoop, calls=%fused_computation | loop fusion | flops 720896 | bytes 1048576 | tf_op jit(solution)/shard_map/reduce_sum | solution.py:469
